TPU v7x, 32 devices: a whole 2x2x4 slice. The times are simulated.
32 devices in a mesh: gx: 4 (over x, core), gy: 8 (over z, y).
Axes of the slice: x: 2, y: 2, z: 4, core: 2. Of those that a mesh axis runs over, the one named last changes fastest.
Arguments:
- source: bfloat16 [16, 512, 256], P(None, ('gx', 'gy')), may hold values from -6 to 6
- leaf_flux: bfloat16 [32768, 256], P(('gx', 'gy')), may hold values from -0.375 to 0.375
- leaf_particular: bfloat16 [131072, 256], P(('gx', 'gy')), may hold values from -0.375 to 0.375
- leaf_lift: bfloat16 [32768, 256], P(('gx', 'gy')), may hold values from -0.75 to 0.75
- box_up: bfloat16 [20480, 1024], P(('gx', 'gy')), may hold values from -0.1875 to 0.1875
- box_down: bfloat16 [32768, 640], P(('gx', 'gy')), may hold values from -0.25 to 0.25
- up_one: bfloat16 [8192, 768], P(('gx', 'gy')), may hold values from -0.1875 to 0.1875
- down_one: bfloat16 [8192, 768], P(('gx', 'gy')), may hold values from -0.21875 to 0.21875
- up_two: bfloat16 [4096, 1536], P(('gx', 'gy')), may hold values from -0.125 to 0.125
- down_two: bfloat16 [4096, 1536], P(('gx', 'gy')), may hold values from -0.15625 to 0.15625
- up_root: bfloat16 [2048, 256], P(('gx', 'gy')), may hold values from -0.125 to 0.125
- down_root: bfloat16 [2048, 256], P(('gx', 'gy')), may hold values from -0.375 to 0.375
Outputs:
- solution: float32 [16, 512, 256], P(None, ('gx', 'gy'))
All inputs are finite; a program needn't handle non-finite values.
Results may differ from a plain program's by a relative error of at most 0.014.
Values may be sent and summed in bfloat16 or wider, within the bound.
No kernel may reach another device: no remote copies, remote signals or barrier semaphores. Data moves between devices by JAX's collectives and lax.ppermute only.
A program may use at most 64 MiB of HBM per device.

v0:
```python
import jax
import jax.numpy as jnp
from jax import lax
from jax.sharding import PartitionSpec as P


def partner(x, axis, stride):
    return lax.ppermute(x, axis, [(i, i ^ 1 << stride) for i in range(lax.axis_size(axis))])


def contract(left, right):
    return lax.dot_general(
        left, right, (((1,), (1,)), ((), ())), preferred_element_type=jnp.float32
    )


def place_pair(joined, other, place, bit_num):
    upper = place // 2**bit_num % 2 == 1
    lower = jnp.where(upper, other, joined)
    higher = jnp.where(upper, joined, other)
    return jnp.concatenate([lower, higher], axis=1)


def sum_sixteen(term):
    total = term
    for bit_num in range(4):
        total = total + partner(total.astype(jnp.bfloat16), ("gx", "gy"), bit_num).astype(
            total.dtype
        )
    return total


def join_sixteen(piece, place):
    joined = piece
    for bit_num in range(4):
        other = partner(joined, ("gx", "gy"), bit_num)
        joined = place_pair(joined, other, place, bit_num)
    return joined


def per_device(
    source,
    leaf_flux,
    leaf_particular,
    leaf_lift,
    box_up,
    box_down,
    up_one,
    down_one,
    up_two,
    down_two,
    up_root,
    down_root,
):
    rhs_count, leaves, points = source.shape
    edge_count = leaf_flux.shape[0] // leaves
    rows_count = lax.axis_size("gy")
    row_place = lax.axis_index("gy")
    place = lax.axis_index("gx") * rows_count + row_place
    k_zero = up_one.shape[0]
    inner_dev = box_up.shape[0] - k_zero
    second_width = up_two.shape[0]
    root_width = up_root.shape[0]
    flux = jnp.einsum(
        "rlq,leq->rle",
        source,
        leaf_flux.reshape(leaves, edge_count, points),
        preferred_element_type=jnp.float32,
    )
    flux = flux.astype(jnp.bfloat16).reshape(rhs_count, leaves * edge_count)
    box_state = contract(flux, box_up).astype(jnp.bfloat16)
    first_term = jnp.dot(box_state[:, inner_dev:], up_one, preferred_element_type=jnp.float32)
    first_sum = first_term
    for bit_num in range(2):
        first_sum = first_sum + partner(first_sum.astype(jnp.bfloat16), "gy", bit_num).astype(
            first_sum.dtype
        )
    first_state = first_sum.astype(jnp.bfloat16)
    k_one = first_state.shape[1] - k_zero
    second_piece = lax.dynamic_slice_in_dim(
        first_state, k_zero + place % 4 * second_width, second_width, 1
    )
    second_term = jnp.dot(second_piece, up_two, preferred_element_type=jnp.float32)
    second_sum = sum_sixteen(second_term)
    second_state = second_sum.astype(jnp.bfloat16)
    root_piece = lax.dynamic_slice_in_dim(
        second_state, k_one + place % 16 * root_width, root_width, 1
    )
    root_term = jnp.dot(root_piece, up_root, preferred_element_type=jnp.float32)
    root_state = lax.psum(root_term, ("gx", "gy")).astype(jnp.bfloat16)
    top_piece = contract(root_state, down_root).astype(jnp.bfloat16)
    top_bound = join_sixteen(top_piece, place)
    second_input = jnp.concatenate([second_state[:, :k_one], top_bound], axis=1)
    mid_piece = contract(second_input, down_two).astype(jnp.bfloat16)
    mid_bound = mid_piece
    for bit_num in range(2):
        other = partner(mid_bound, "gy", bit_num)
        mid_bound = place_pair(mid_bound, other, place, bit_num)
    first_input = jnp.concatenate([first_state[:, :k_zero], mid_bound], axis=1)
    box_bound = contract(first_input, down_one).astype(jnp.bfloat16)
    box_input = jnp.concatenate([box_state[:, :inner_dev], box_bound], axis=1)
    leaf_bound = (
        contract(box_input, box_down).astype(jnp.bfloat16).reshape(rhs_count, leaves, edge_count)
    )
    lifted = jnp.einsum(
        "rle,leq->rlq",
        leaf_bound,
        leaf_lift.reshape(leaves, edge_count, points),
        preferred_element_type=jnp.float32,
    )
    particular = jnp.einsum(
        "rlq,lqp->rlp",
        source,
        leaf_particular.reshape(leaves, points, points),
        preferred_element_type=jnp.float32,
    )
    return lifted + particular


def solution(mesh):
    return jax.shard_map(
        per_device,
        mesh=mesh,
        in_specs=(
            P(None, ("gx", "gy"), None),
            P(("gx", "gy"), None),
            P(("gx", "gy"), None),
            P(("gx", "gy"), None),
            P(("gx", "gy"), None),
            P(("gx", "gy"), None),
            P(("gx", "gy"), None),
            P(("gx", "gy"), None),
            P(("gx", "gy"), None),
            P(("gx", "gy"), None),
            P(("gx", "gy"), None),
            P(("gx", "gy"), None),
        ),
        out_specs=P(None, ("gx", "gy"), None),
        check_vma=False,
    )
```

profile of v0, /device:TPU:0, one launch (start us, length us, event | category | flops | bytes accessed | tf_op | source)
XLA Modules:
  0.0 91.7 jit_solution(6678970765712503104)
XLA Ops:
  0.0 0.0 copy-start
  0.0 0.0 copy-start.7
  0.0 1.4 %fusion.1 = bf16[16,16,64]{2,0,1:T(8,128)(2,1)S(1)} fusion(bf16[16,64,256]{2,1,0:T(8,128)(2,1)} %bitcast.25, bf16[16,16,256]{2,1,0:T(8,128)(2,1)} %param.12), kind=kOutput, calls=%fused_computation.4 | convolution fusion | flops 8404992 | bytes 688128 | tf_op jit(solution)/shard_map/rlq,leq->rle/dot_general | solution.py:64
  1.5 0.0 copy-start.4
  1.5 0.1 reshape.16
  1.6 1.8 %convolution_convert_fusion.2 = bf16[16,640]{1,0:T(8,128)(2,1)S(1)} fusion(bf16[16,1024]{1,0:T(8,128)(2,1)S(1)} %reshape.16, bf16[640,1024]{1,0:T(8,128)(2,1)} %param.16), kind=kOutput, calls=%fused_computation.6 | convolution fusion | flops 20981760 | bytes 1363968 | tf_op jit(solution)/shard_map/dot_general | solution.py:12
  3.4 0.0 copy-done.7
  3.4 0.0 copy-start.8
  3.4 0.0 copy-start.9
  3.4 0.2 fusion.34
  3.6 0.0 copy-start.5
  3.6 3.0 %collective-permute-start = (bf16[16,768]{1,0:T(8,128)(2,1)S(1)}, bf16[16,768]{1,0:T(8,128)(2,1)S(1)}, u32[]{:S(2)}, u32[]{:S(2)}) collective-permute-start(bf16[16,768]{1,0:T(8,128)(2,1)S(1)} %get-tuple-element.17), channel_id=1, source_target_pairs={{0,1},{1,0},{2,3},{3,2},{4,5},{5,4},{6,7},{7,6},{8,9},{9,8},{10,11... | collective-permute-start | bytes 73736 | tf_op jit(solution)/shard_map/ppermute | solution.py:8
  6.6 1.8 %collective-permute-done = bf16[16,768]{1,0:T(8,128)(2,1)S(1)} collective-permute-done((bf16[16,768]{1,0:T(8,128)(2,1)S(1)}, bf16[16,768]{1,0:T(8,128)(2,1)S(1)}, u32[]{:S(2)}, u32[]{:S(2)}) %collective-permute-start) | collective-permute-done | bytes 24608 | tf_op jit(solution)/shard_map/ppermute | solution.py:8
  8.4 2.1 %collective-permute-start.1 = (bf16[16,768]{1,0:T(8,128)(2,1)S(1)}, bf16[16,768]{1,0:T(8,128)(2,1)S(1)}, u32[]{:S(2)}, u32[]{:S(2)}) collective-permute-start(bf16[16,768]{1,0:T(8,128)(2,1)S(1)} %fusion.12), channel_id=1, source_target_pairs={{0,2},{1,3},{2,0},{3,1},{4,6},{5,7},{6,4},{7,5},{8,10},{9,11},{10,... | collective-permute-start | bytes 73736 | tf_op jit(solution)/shard_map/ppermute | solution.py:8
  10.6 1.8 %collective-permute-done.1 = bf16[16,768]{1,0:T(8,128)(2,1)S(1)} collective-permute-done((bf16[16,768]{1,0:T(8,128)(2,1)S(1)}, bf16[16,768]{1,0:T(8,128)(2,1)S(1)}, u32[]{:S(2)}, u32[]{:S(2)}) %collective-permute-start.1) | collective-permute-done | bytes 24608 | tf_op jit(solution)/shard_map/ppermute | solution.py:8
  12.4 0.0 copy-done.4
  12.4 0.0 copy-start.3
  12.4 0.2 fusion.35
  12.6 2.0 %collective-permute-start.2 = (bf16[16,1536]{1,0:T(8,128)(2,1)S(1)}, bf16[16,1536]{1,0:T(8,128)(2,1)S(1)}, u32[]{:S(2)}, u32[]{:S(2)}) collective-permute-start(bf16[16,1536]{1,0:T(8,128)(2,1)S(1)} %get-tuple-element.19), channel_id=1, source_target_pairs={{0,1},{1,0},{2,3},{3,2},{4,5},{5,4},{6,7},{7,6},{8,9},{9,8},{10,11... | collective-permute-start | bytes 147464 | tf_op jit(solution)/shard_map/ppermute | solution.py:8
  14.6 2.1 %collective-permute-done.2 = bf16[16,1536]{1,0:T(8,128)(2,1)S(1)} collective-permute-done((bf16[16,1536]{1,0:T(8,128)(2,1)S(1)}, bf16[16,1536]{1,0:T(8,128)(2,1)S(1)}, u32[]{:S(2)}, u32[]{:S(2)}) %collective-permute-start.2) | collective-permute-done | bytes 49184 | tf_op jit(solution)/shard_map/ppermute | solution.py:8
  16.7 2.1 %collective-permute-start.3 = (bf16[16,1536]{1,0:T(8,128)(2,1)S(1)}, bf16[16,1536]{1,0:T(8,128)(2,1)S(1)}, u32[]{:S(2)}, u32[]{:S(2)}) collective-permute-start(bf16[16,1536]{1,0:T(8,128)(2,1)S(1)} %fusion.4), channel_id=1, source_target_pairs={{0,2},{1,3},{2,0},{3,1},{4,6},{5,7},{6,4},{7,5},{8,10},{9,11},{10,... | collective-permute-start | bytes 147464 | tf_op jit(solution)/shard_map/ppermute | solution.py:8
  18.8 2.6 %collective-permute-done.3 = bf16[16,1536]{1,0:T(8,128)(2,1)S(1)} collective-permute-done((bf16[16,1536]{1,0:T(8,128)(2,1)S(1)}, bf16[16,1536]{1,0:T(8,128)(2,1)S(1)}, u32[]{:S(2)}, u32[]{:S(2)}) %collective-permute-start.3) | collective-permute-done | bytes 49184 | tf_op jit(solution)/shard_map/ppermute | solution.py:8
  21.4 2.6 %collective-permute-start.4 = (bf16[16,1536]{1,0:T(8,128)(2,1)S(1)}, bf16[16,1536]{1,0:T(8,128)(2,1)S(1)}, u32[]{:S(2)}, u32[]{:S(2)}) collective-permute-start(bf16[16,1536]{1,0:T(8,128)(2,1)S(1)} %fusion.33), channel_id=1, source_target_pairs={{0,4},{1,5},{2,6},{3,7},{4,0},{5,1},{6,2},{7,3},{8,12},{9,13},{10,... | collective-permute-start | bytes 147464 | tf_op jit(solution)/shard_map/ppermute | solution.py:8
  24.0 2.5 %collective-permute-done.4 = bf16[16,1536]{1,0:T(8,128)(2,1)S(1)} collective-permute-done((bf16[16,1536]{1,0:T(8,128)(2,1)S(1)}, bf16[16,1536]{1,0:T(8,128)(2,1)S(1)}, u32[]{:S(2)}, u32[]{:S(2)}) %collective-permute-start.4) | collective-permute-done | bytes 49184 | tf_op jit(solution)/shard_map/ppermute | solution.py:8
  26.5 0.1 collective-permute-start.5
  26.6 1.2 %collective-permute-done.5 = bf16[16,1536]{1,0:T(8,128)(2,1)S(1)} collective-permute-done((bf16[16,1536]{1,0:T(8,128)(2,1)S(1)}, bf16[16,1536]{1,0:T(8,128)(2,1)S(1)}, u32[]{:S(2)}, u32[]{:S(2)}) %collective-permute-start.5) | collective-permute-done | bytes 49184 | tf_op jit(solution)/shard_map/ppermute | solution.py:8
  27.8 0.0 copy-done.8
  27.9 0.2 fusion.24
  28.1 40.5 %psum.7 = bf16[16,256]{1,0:T(8,128)(2,1)S(1)} all-reduce(f32[16,256]{1,0:T(8,128)S(1)} %fusion.24), channel_id=1, replica_groups=mesh['gx'=4,'gy'=8] {'gx','gy'}, use_global_device_ids=true, to_apply=%region_0.1 | all-reduce | flops 4096 | bytes 24576 | tf_op jit(solution)/shard_map/psum | solution.py:90
  68.5 0.0 copy-done.9
  68.6 0.1 convolution_convert_fusion.4
  68.7 2.3 %collective-permute-start.6 = (bf16[16,64]{1,0:T(8,128)(2,1)S(1)}, bf16[16,64]{1,0:T(8,128)(2,1)S(1)}, u32[]{:S(2)}, u32[]{:S(2)}) collective-permute-start(bf16[16,64]{1,0:T(8,128)(2,1)S(1)} %convolution_convert_fusion.4), channel_id=1, source_target_pairs={{0,1},{1,0},{2,3},{3,2},{4,5},{5,4},{6,7},{7,6},{8,9},{9,8},{10,11... | collective-permute-start | bytes 6152 | tf_op jit(solution)/shard_map/ppermute | solution.py:8
  71.0 1.6 %collective-permute-done.6 = bf16[16,64]{1,0:T(8,128)(2,1)S(1)} collective-permute-done((bf16[16,64]{1,0:T(8,128)(2,1)S(1)}, bf16[16,64]{1,0:T(8,128)(2,1)S(1)}, u32[]{:S(2)}, u32[]{:S(2)}) %collective-permute-start.6) | collective-permute-done | bytes 2080 | tf_op jit(solution)/shard_map/ppermute | solution.py:8
  72.6 0.1 pad_maximum_fusion.3
  72.7 1.9 %collective-permute-start.7 = (bf16[16,128]{1,0:T(8,128)(2,1)S(1)}, bf16[16,128]{1,0:T(8,128)(2,1)S(1)}, u32[]{:S(2)}, u32[]{:S(2)}) collective-permute-start(bf16[16,128]{1,0:T(8,128)(2,1)S(1)} %pad_maximum_fusion.3), channel_id=1, source_target_pairs={{0,2},{1,3},{2,0},{3,1},{4,6},{5,7},{6,4},{7,5},{8,10},{9,11},{10,... | collective-permute-start | bytes 12296 | tf_op jit(solution)/shard_map/ppermute | solution.py:8
  74.6 1.7 %collective-permute-done.7 = bf16[16,128]{1,0:T(8,128)(2,1)S(1)} collective-permute-done((bf16[16,128]{1,0:T(8,128)(2,1)S(1)}, bf16[16,128]{1,0:T(8,128)(2,1)S(1)}, u32[]{:S(2)}, u32[]{:S(2)}) %collective-permute-start.7) | collective-permute-done | bytes 4128 | tf_op jit(solution)/shard_map/ppermute | solution.py:8
  76.3 0.1 broadcast_select_fusion.9
  76.4 2.7 %collective-permute-start.8 = (bf16[16,256]{1,0:T(8,128)(2,1)S(1)}, bf16[16,256]{1,0:T(8,128)(2,1)S(1)}, u32[]{:S(2)}, u32[]{:S(2)}) collective-permute-start(bf16[16,256]{1,0:T(8,128)(2,1)S(1)} %pad_maximum_fusion.1), channel_id=1, source_target_pairs={{0,4},{1,5},{2,6},{3,7},{4,0},{5,1},{6,2},{7,3},{8,12},{9,13},{10,... | collective-permute-start | bytes 24584 | tf_op jit(solution)/shard_map/ppermute | solution.py:8
  79.1 1.8 %collective-permute-done.8 = bf16[16,256]{1,0:T(8,128)(2,1)S(1)} collective-permute-done((bf16[16,256]{1,0:T(8,128)(2,1)S(1)}, bf16[16,256]{1,0:T(8,128)(2,1)S(1)}, u32[]{:S(2)}, u32[]{:S(2)}) %collective-permute-start.8) | collective-permute-done | bytes 8224 | tf_op jit(solution)/shard_map/ppermute | solution.py:8
  80.9 0.1 collective-permute-start.9
  81.0 1.1 %collective-permute-done.9 = bf16[16,512]{1,0:T(8,128)(2,1)S(1)} collective-permute-done((bf16[16,512]{1,0:T(8,128)(2,1)S(1)}, bf16[16,512]{1,0:T(8,128)(2,1)S(1)}, u32[]{:S(2)}, u32[]{:S(2)}) %collective-permute-start.9) | collective-permute-done | bytes 16416 | tf_op jit(solution)/shard_map/ppermute | solution.py:8
  82.2 0.0 copy-done.5
  82.2 0.2 convolution_convert_fusion.5
  82.4 0.0 copy-start.6
  82.4 2.1 %collective-permute-start.10 = (bf16[16,128]{1,0:T(8,128)(2,1)S(1)}, bf16[16,128]{1,0:T(8,128)(2,1)S(1)}, u32[]{:S(2)}, u32[]{:S(2)}) collective-permute-start(bf16[16,128]{1,0:T(8,128)(2,1)S(1)} %convolution_convert_fusion.5), channel_id=1, source_target_pairs={{0,1},{1,0},{2,3},{3,2},{4,5},{5,4},{6,7},{7,6},{8,9},{9,8},{10,11... | collective-permute-start | bytes 12296 | tf_op jit(solution)/shard_map/ppermute | solution.py:8
  84.4 1.6 %collective-permute-done.10 = bf16[16,128]{1,0:T(8,128)(2,1)S(1)} collective-permute-done((bf16[16,128]{1,0:T(8,128)(2,1)S(1)}, bf16[16,128]{1,0:T(8,128)(2,1)S(1)}, u32[]{:S(2)}, u32[]{:S(2)}) %collective-permute-start.10) | collective-permute-done | bytes 4128 | tf_op jit(solution)/shard_map/ppermute | solution.py:8
  86.0 2.0 %collective-permute-start.11 = (bf16[16,256]{1,0:T(8,128)(2,1)S(1)}, bf16[16,256]{1,0:T(8,128)(2,1)S(1)}, u32[]{:S(2)}, u32[]{:S(2)}) collective-permute-start(bf16[16,256]{1,0:T(8,128)(2,1)S(1)} %pad_maximum_fusion.2), channel_id=1, source_target_pairs={{0,2},{1,3},{2,0},{3,1},{4,6},{5,7},{6,4},{7,5},{8,10},{9,11},{10,... | collective-permute-start | bytes 24584 | tf_op jit(solution)/shard_map/ppermute | solution.py:8
  88.1 0.0 copy-done
  88.1 0.0 copy-done.3
  88.1 0.0 copy-start.1
  88.1 0.4 convolution_bitcast_fusion.1
  88.4 0.0 copy-start.2
  88.5 1.3 %collective-permute-done.11 = bf16[16,256]{1,0:T(8,128)(2,1)S(1)} collective-permute-done((bf16[16,256]{1,0:T(8,128)(2,1)S(1)}, bf16[16,256]{1,0:T(8,128)(2,1)S(1)}, u32[]{:S(2)}, u32[]{:S(2)}) %collective-permute-start.11) | collective-permute-done | bytes 8224 | tf_op jit(solution)/shard_map/ppermute | solution.py:8
  89.8 0.0 copy-done.6
  89.8 0.2 convolution_convert_fusion.3
  89.9 0.0 copy-done.1
  89.9 0.5 convolution_convert_fusion.1
  90.5 0.1 reshape.17
  90.6 0.0 copy-done.2
  90.6 0.2 fusion
  90.8 0.9 copy.21
  (18 shorter events, 0.2 us)
Async XLA Ops:
  0.0 88.1 %copy-start = (bf16[4096,256]{1,0:T(8,128)(2,1)S(1)}, bf16[4096,256]{1,0:T(8,128)(2,1)}, u32[]{:S(2)}) copy-start(bf16[4096,256]{1,0:T(8,128)(2,1)} %param.14) | copy-start | bytes 6291460
  0.0 3.4 %copy-start.7 = (bf16[256,768]{1,0:T(8,128)(2,1)S(1)}, bf16[256,768]{1,0:T(8,128)(2,1)}, u32[]{:S(2)}) copy-start(bf16[256,768]{1,0:T(8,128)(2,1)} %param.18) | copy-start | bytes 1179652
  1.5 10.9 %copy-start.4 = (bf16[128,1536]{1,0:T(8,128)(2,1)S(1)}, bf16[128,1536]{1,0:T(8,128)(2,1)}, u32[]{:S(2)}) copy-start(bf16[128,1536]{1,0:T(8,128)(2,1)} %param.20) | copy-start | bytes 1179652
  3.4 24.5 %copy-start.8 = (bf16[64,256]{1,0:T(8,128)(2,1)S(1)}, bf16[64,256]{1,0:T(8,128)(2,1)}, u32[]{:S(2)}) copy-start(bf16[64,256]{1,0:T(8,128)(2,1)} %param.22) | copy-start | bytes 98308
  3.4 65.2 %copy-start.9 = (bf16[64,256]{1,0:T(8,128)(2,1)S(1)}, bf16[64,256]{1,0:T(8,128)(2,1)}, u32[]{:S(2)}) copy-start(bf16[64,256]{1,0:T(8,128)(2,1)} %param.23) | copy-start | bytes 98308
  3.6 78.6 %copy-start.5 = (bf16[128,1536]{1,0:T(8,128)(2,1)S(1)}, bf16[128,1536]{1,0:T(8,128)(2,1)}, u32[]{:S(2)}) copy-start(bf16[128,1536]{1,0:T(8,128)(2,1)} %param.21) | copy-start | bytes 1179652
  3.6 4.8 %collective-permute-start = (bf16[16,768]{1,0:T(8,128)(2,1)S(1)}, bf16[16,768]{1,0:T(8,128)(2,1)S(1)}, u32[]{:S(2)}, u32[]{:S(2)}) collective-permute-start(bf16[16,768]{1,0:T(8,128)(2,1)S(1)} %get-tuple-element.17), channel_id=1, source_target_pairs={{0,1},{1,0},{2,3},{3,2},{4,5},{5,4},{6,7},{7,6},{8,9},{9,8},{10,11... | collective-permute-start | bytes 73736 | tf_op jit(solution)/shard_map/ppermute | solution.py:8
  8.4 3.9 %collective-permute-start.1 = (bf16[16,768]{1,0:T(8,128)(2,1)S(1)}, bf16[16,768]{1,0:T(8,128)(2,1)S(1)}, u32[]{:S(2)}, u32[]{:S(2)}) collective-permute-start(bf16[16,768]{1,0:T(8,128)(2,1)S(1)} %fusion.12), channel_id=1, source_target_pairs={{0,2},{1,3},{2,0},{3,1},{4,6},{5,7},{6,4},{7,5},{8,10},{9,11},{10,... | collective-permute-start | bytes 73736 | tf_op jit(solution)/shard_map/ppermute | solution.py:8
  12.4 75.7 %copy-start.3 = (bf16[16,16,256]{2,1,0:T(8,128)(2,1)S(1)}, bf16[16,16,256]{2,1,0:T(8,128)(2,1)}, u32[]{:S(2)}) copy-start(bf16[16,16,256]{2,1,0:T(8,128)(2,1)} %param.12) | copy-start | bytes 393220
  12.6 4.1 %collective-permute-start.2 = (bf16[16,1536]{1,0:T(8,128)(2,1)S(1)}, bf16[16,1536]{1,0:T(8,128)(2,1)S(1)}, u32[]{:S(2)}, u32[]{:S(2)}) collective-permute-start(bf16[16,1536]{1,0:T(8,128)(2,1)S(1)} %get-tuple-element.19), channel_id=1, source_target_pairs={{0,1},{1,0},{2,3},{3,2},{4,5},{5,4},{6,7},{7,6},{8,9},{9,8},{10,11... | collective-permute-start | bytes 147464 | tf_op jit(solution)/shard_map/ppermute | solution.py:8
  16.7 4.7 %collective-permute-start.3 = (bf16[16,1536]{1,0:T(8,128)(2,1)S(1)}, bf16[16,1536]{1,0:T(8,128)(2,1)S(1)}, u32[]{:S(2)}, u32[]{:S(2)}) collective-permute-start(bf16[16,1536]{1,0:T(8,128)(2,1)S(1)} %fusion.4), channel_id=1, source_target_pairs={{0,2},{1,3},{2,0},{3,1},{4,6},{5,7},{6,4},{7,5},{8,10},{9,11},{10,... | collective-permute-start | bytes 147464 | tf_op jit(solution)/shard_map/ppermute | solution.py:8
  21.4 5.1 %collective-permute-start.4 = (bf16[16,1536]{1,0:T(8,128)(2,1)S(1)}, bf16[16,1536]{1,0:T(8,128)(2,1)S(1)}, u32[]{:S(2)}, u32[]{:S(2)}) collective-permute-start(bf16[16,1536]{1,0:T(8,128)(2,1)S(1)} %fusion.33), channel_id=1, source_target_pairs={{0,4},{1,5},{2,6},{3,7},{4,0},{5,1},{6,2},{7,3},{8,12},{9,13},{10,... | collective-permute-start | bytes 147464 | tf_op jit(solution)/shard_map/ppermute | solution.py:8
  26.5 1.3 %collective-permute-start.5 = (bf16[16,1536]{1,0:T(8,128)(2,1)S(1)}, bf16[16,1536]{1,0:T(8,128)(2,1)S(1)}, u32[]{:S(2)}, u32[]{:S(2)}) collective-permute-start(bf16[16,1536]{1,0:T(8,128)(2,1)S(1)} %fusion.5), channel_id=1, source_target_pairs={{0,8},{1,9},{2,10},{3,11},{4,12},{5,13},{6,14},{7,15},{8,0},{9,1},... | collective-permute-start | bytes 147464 | tf_op jit(solution)/shard_map/ppermute | solution.py:8
  68.7 3.9 %collective-permute-start.6 = (bf16[16,64]{1,0:T(8,128)(2,1)S(1)}, bf16[16,64]{1,0:T(8,128)(2,1)S(1)}, u32[]{:S(2)}, u32[]{:S(2)}) collective-permute-start(bf16[16,64]{1,0:T(8,128)(2,1)S(1)} %convolution_convert_fusion.4), channel_id=1, source_target_pairs={{0,1},{1,0},{2,3},{3,2},{4,5},{5,4},{6,7},{7,6},{8,9},{9,8},{10,11... | collective-permute-start | bytes 6152 | tf_op jit(solution)/shard_map/ppermute | solution.py:8
  72.7 3.6 %collective-permute-start.7 = (bf16[16,128]{1,0:T(8,128)(2,1)S(1)}, bf16[16,128]{1,0:T(8,128)(2,1)S(1)}, u32[]{:S(2)}, u32[]{:S(2)}) collective-permute-start(bf16[16,128]{1,0:T(8,128)(2,1)S(1)} %pad_maximum_fusion.3), channel_id=1, source_target_pairs={{0,2},{1,3},{2,0},{3,1},{4,6},{5,7},{6,4},{7,5},{8,10},{9,11},{10,... | collective-permute-start | bytes 12296 | tf_op jit(solution)/shard_map/ppermute | solution.py:8
  76.4 4.6 %collective-permute-start.8 = (bf16[16,256]{1,0:T(8,128)(2,1)S(1)}, bf16[16,256]{1,0:T(8,128)(2,1)S(1)}, u32[]{:S(2)}, u32[]{:S(2)}) collective-permute-start(bf16[16,256]{1,0:T(8,128)(2,1)S(1)} %pad_maximum_fusion.1), channel_id=1, source_target_pairs={{0,4},{1,5},{2,6},{3,7},{4,0},{5,1},{6,2},{7,3},{8,12},{9,13},{10,... | collective-permute-start | bytes 24584 | tf_op jit(solution)/shard_map/ppermute | solution.py:8
  80.9 1.2 %collective-permute-start.9 = (bf16[16,512]{1,0:T(8,128)(2,1)S(1)}, bf16[16,512]{1,0:T(8,128)(2,1)S(1)}, u32[]{:S(2)}, u32[]{:S(2)}) collective-permute-start(bf16[16,512]{1,0:T(8,128)(2,1)S(1)} %pad_maximum_fusion), channel_id=1, source_target_pairs={{0,8},{1,9},{2,10},{3,11},{4,12},{5,13},{6,14},{7,15},{8,0},{9,1},... | collective-permute-start | bytes 49160 | tf_op jit(solution)/shard_map/ppermute | solution.py:8
  82.4 7.4 %copy-start.6 = (bf16[256,768]{1,0:T(8,128)(2,1)S(1)}, bf16[256,768]{1,0:T(8,128)(2,1)}, u32[]{:S(2)}) copy-start(bf16[256,768]{1,0:T(8,128)(2,1)} %param.19) | copy-start | bytes 1179652
  82.4 3.6 %collective-permute-start.10 = (bf16[16,128]{1,0:T(8,128)(2,1)S(1)}, bf16[16,128]{1,0:T(8,128)(2,1)S(1)}, u32[]{:S(2)}, u32[]{:S(2)}) collective-permute-start(bf16[16,128]{1,0:T(8,128)(2,1)S(1)} %convolution_convert_fusion.5), channel_id=1, source_target_pairs={{0,1},{1,0},{2,3},{3,2},{4,5},{5,4},{6,7},{7,6},{8,9},{9,8},{10,11... | collective-permute-start | bytes 12296 | tf_op jit(solution)/shard_map/ppermute | solution.py:8
  86.0 3.7 %collective-permute-start.11 = (bf16[16,256]{1,0:T(8,128)(2,1)S(1)}, bf16[16,256]{1,0:T(8,128)(2,1)S(1)}, u32[]{:S(2)}, u32[]{:S(2)}) collective-permute-start(bf16[16,256]{1,0:T(8,128)(2,1)S(1)} %pad_maximum_fusion.2), channel_id=1, source_target_pairs={{0,2},{1,3},{2,0},{3,1},{4,6},{5,7},{6,4},{7,5},{8,10},{9,11},{10,... | collective-permute-start | bytes 24584 | tf_op jit(solution)/shard_map/ppermute | solution.py:8
  88.1 1.9 %copy-start.1 = (bf16[1024,640]{1,0:T(8,128)(2,1)S(1)}, bf16[1024,640]{1,0:T(8,128)(2,1)}, u32[]{:S(2)}) copy-start(bf16[1024,640]{1,0:T(8,128)(2,1)} %param.17) | copy-start | bytes 3932164
  88.4 2.2 %copy-start.2 = (bf16[1024,256]{1,0:T(8,128)(2,1)S(1)}, bf16[1024,256]{1,0:T(8,128)(2,1)}, u32[]{:S(2)}) copy-start(bf16[1024,256]{1,0:T(8,128)(2,1)} %param.15) | copy-start | bytes 1572868
where the time goes:
time: 91.9 us; the launch traced here: 91.7 us
  blocking collectives  40.5 us (44%)
  starting transfers between devices  23 us (25%)
  waiting for transfers between devices  21.1 us (23%)
  matrix products  5.3 us (6%)
  local copies, waits for them, and re-layouts  1.2 us (1%)
    psum x1, blocking collectives, per_device(): root_state = lax.psum(root_term, ('gx', 'gy')).astype(jnp.bfloat16)  40.5 us
    ppermute x12, starting transfers between devices, partner(): lax.ppermute(x, axis, [(i, i ^ 1 << stride) for i in range(lax.axis_size(...  23 us
    ppermute x12, waiting for transfers between devices, partner(): lax.ppermute(x, axis, [(i, i ^ 1 << stride) for i in range(lax.axis_size(...  21.1 us
    dot_general x5, matrix products, contract(): lax.dot_general(left, right, (((1,), (1,)), ((), ())), preferred_element_...  2.76 us
  transfers between devices with their start and end apart: 12, of which 12 were waited for; matrix products, arithmetic and copies ran while one was open for 0% of the time, Pallas kernels for 0%

commit v1 on v0

v1 whole, which is shorter than its diff:
```python
import jax
import jax.numpy as jnp
from jax import lax
from jax.sharding import PartitionSpec as P

AXES = ("gx", "gy")


def contract(left, right):
    return lax.dot_general(
        left, right, (((1,), (1,)), ((), ())), preferred_element_type=jnp.float32
    )


def groups_of(size):
    count = lax.axis_size(AXES)
    return [list(range(start, start + size)) for start in range(0, count, size)]


def swap(pieces, size):
    return lax.all_to_all(pieces, AXES, 0, 0, axis_index_groups=groups_of(size))


def per_device(
    source,
    leaf_flux,
    leaf_particular,
    leaf_lift,
    box_up,
    box_down,
    up_one,
    down_one,
    up_two,
    down_two,
    up_root,
    down_root,
):
    rhs_count, leaves, points = source.shape
    edge_count = leaf_flux.shape[0] // leaves
    count = lax.axis_size(AXES)
    k_zero = up_one.shape[0]
    inner_dev = box_up.shape[0] - k_zero
    second_width = up_two.shape[0]
    first_inner = k_zero
    quad = (up_one.shape[1] - first_inner) // second_width
    k_one = up_one.shape[1] - first_inner
    root_width = up_root.shape[0]
    family = (up_two.shape[1] - k_one) // root_width

    root_up_all = lax.all_gather(
        up_root, AXES, axis_index_groups=groups_of(family), tiled=True
    )
    root_down_all = lax.all_gather(
        down_root, AXES, axis_index_groups=groups_of(family), tiled=True
    )

    flux = jnp.einsum(
        "rlq,leq->rle",
        source,
        leaf_flux.reshape(leaves, edge_count, points),
        preferred_element_type=jnp.float32,
    )
    flux = flux.astype(jnp.bfloat16).reshape(rhs_count, leaves * edge_count)
    box_state = contract(flux, box_up).astype(jnp.bfloat16)
    first_term = jnp.dot(box_state[:, inner_dev:], up_one, preferred_element_type=jnp.float32)
    first_term = first_term.astype(jnp.bfloat16)
    outer = first_term[:, first_inner:].reshape(rhs_count, quad, second_width).swapaxes(0, 1)
    inner = jnp.broadcast_to(first_term[:, :first_inner], (quad, rhs_count, first_inner))
    got = swap(jnp.concatenate([outer, inner], axis=2), quad)
    first_sum = jnp.sum(got.astype(jnp.float32), axis=0).astype(jnp.bfloat16)
    second_piece = first_sum[:, :second_width]
    first_inner_state = first_sum[:, second_width:]

    up_short = jnp.dot(
        up_two[:, k_one:], root_up_all, preferred_element_type=jnp.float32
    ).astype(jnp.bfloat16)
    down_short = jnp.dot(
        down_two[:, k_one:], root_down_all, preferred_element_type=jnp.float32
    ).astype(jnp.bfloat16)

    second_term = jnp.dot(
        second_piece, jnp.concatenate([up_two[:, :k_one], up_short], axis=1),
        preferred_element_type=jnp.float32,
    ).astype(jnp.bfloat16)
    rows = rhs_count // family
    got = swap(second_term.reshape(family, rows, second_term.shape[1]), family)
    second_rows = jnp.sum(got.astype(jnp.float32), axis=0)
    second_all = lax.all_to_all(
        jnp.broadcast_to(second_rows, (count,) + second_rows.shape), AXES, 0, 0
    ).reshape(count // family, rhs_count, second_rows.shape[1])
    own = lax.axis_index(AXES) // family
    root_state = jnp.sum(second_all[:, :, k_one:], axis=0).astype(jnp.bfloat16)
    second_inner = lax.dynamic_index_in_dim(
        second_all[:, :, :k_one], own, 0, keepdims=False
    ).astype(jnp.bfloat16)
    mid_piece = contract(
        jnp.concatenate([second_inner, root_state], axis=1),
        jnp.concatenate([down_two[:, :k_one], down_short], axis=1),
    ).astype(jnp.bfloat16)
    mid_bound = swap(jnp.broadcast_to(mid_piece, (quad,) + mid_piece.shape), quad)
    mid_bound = mid_bound.swapaxes(0, 1).reshape(rhs_count, k_one)
    first_input = jnp.concatenate([first_inner_state, mid_bound], axis=1)
    box_bound = contract(first_input, down_one).astype(jnp.bfloat16)
    box_input = jnp.concatenate([box_state[:, :inner_dev], box_bound], axis=1)
    leaf_bound = (
        contract(box_input, box_down).astype(jnp.bfloat16).reshape(rhs_count, leaves, edge_count)
    )
    lifted = jnp.einsum(
        "rle,leq->rlq",
        leaf_bound,
        leaf_lift.reshape(leaves, edge_count, points),
        preferred_element_type=jnp.float32,
    )
    particular = jnp.einsum(
        "rlq,lqp->rlp",
        source,
        leaf_particular.reshape(leaves, points, points),
        preferred_element_type=jnp.float32,
    )
    return lifted + particular


def solution(mesh):
    return jax.shard_map(
        per_device,
        mesh=mesh,
        in_specs=(P(None, AXES, None),) + (P(AXES, None),) * 11,
        out_specs=P(None, AXES, None),
        check_vma=False,
    )
```

time: 91.9 us -> 114 us (1.24)
  blocking collectives: 40.5 us -> 71.5 us
  waiting for transfers between devices: 21.1 us -> 9.64 us
  starting transfers between devices: 23 us -> 15.1 us
  local copies, waits for them, and re-layouts: 1.2 us -> 5.6 us
  matrix products: 5.3 us -> 9.61 us
    all_gather x0 -> x2, blocking collectives: none -> 71.5 us  [the longest x1 36 us: per_device(): lax.all_gather(down_root, AXES, axis_index_groups=groups_of(family), tile...]
    psum x1 -> x0, blocking collectives: 40.5 us -> none  [per_device(): root_state = lax.psum(root_term, ('gx', 'gy')).astype(jnp.bfloat16)]
    ppermute x12 -> x0, starting transfers between devices: 23 us -> none  [partner(): lax.ppermute(x, axis, [(i, i ^ 1 << stride) for i in range(lax.axis_size(...]
    ppermute x12 -> x0, waiting for transfers between devices: 21.1 us -> none  [partner(): lax.ppermute(x, axis, [(i, i ^ 1 << stride) for i in range(lax.axis_size(...]
    all_to_all x0 -> x4, starting transfers between devices: none -> 15.1 us  [the longest x3 12.6 us: swap(): return lax.all_to_all(pieces, AXES, 0, 0, axis_index_groups=groups_of(size))]
    all_to_all x0 -> x4, waiting for transfers between devices: none -> 9.64 us  [the longest x1 6.69 us: per_device(): lax.all_to_all(jnp.broadcast_to(second_rows, (count,) + second_rows.shape...]
    dot_general x5 -> x4, matrix products: 2.76 us -> 4.38 us  [contract(): lax.dot_general(left, right, (((1,), (1,)), ((), ())), preferred_element_...]
    broadcast_in_dim x0 -> x3, local copies, waits for them, and re-layouts: none -> 1.36 us  [the longest x1 0.69 us: per_device(): jnp.broadcast_to(second_rows, (count,) + second_rows.shape)]
  transfers between devices with their start and end apart: 12 -> 4, of which waited for: 12 -> 2; matrix products, arithmetic and copies ran while one was open for 0% -> 3% of each run, Pallas kernels for 0% -> 0%
where the time goes in v1:
time: 114 us; the launch traced here: 113 us
  blocking collectives  71.5 us (63%)
  starting transfers between devices  15.1 us (13%)
  waiting for transfers between devices  9.64 us (8%)
  matrix products  9.61 us (8%)
  local copies, waits for them, and re-layouts  5.6 us (5%)
  other arithmetic  1.4 us (1%)
    all_gather x1, blocking collectives, per_device(): lax.all_gather(down_root, AXES, axis_index_groups=groups_of(family), tile...  36 us
    all_gather x1, blocking collectives, per_device(): lax.all_gather(up_root, AXES, axis_index_groups=groups_of(family), tiled=...  35.5 us
    all_to_all x3, starting transfers between devices, swap(): return lax.all_to_all(pieces, AXES, 0, 0, axis_index_groups=groups_of(size))  12.6 us
    all_to_all x1, waiting for transfers between devices, per_device(): lax.all_to_all(jnp.broadcast_to(second_rows, (count,) + second_rows.shape...  6.69 us
    dot_general x4, matrix products, contract(): lax.dot_general(left, right, (((1,), (1,)), ((), ())), preferred_element_...  4.38 us
    all_to_all x3, waiting for transfers between devices, swap(): return lax.all_to_all(pieces, AXES, 0, 0, axis_index_groups=groups_of(size))  2.94 us
    all_to_all x1, starting transfers between devices, per_device(): lax.all_to_all(jnp.broadcast_to(second_rows, (count,) + second_rows.shape...  2.57 us
  transfers between devices with their start and end apart: 4, of which 2 were waited for; matrix products, arithmetic and copies ran while one was open for 3% of the time, Pallas kernels for 0%

profile of v1, /device:TPU:0, one launch (start us, length us, event | category | flops | bytes accessed | tf_op | source)
XLA Modules:
  0.0 113.2 jit_solution(4486939420531845364)
XLA Ops:
  0.0 0.0 copy-start
  0.0 0.0 copy-start.3
  0.0 1.4 %fusion.1 = bf16[16,16,64]{2,0,1:T(8,128)(2,1)S(1)} fusion(bf16[16,64,256]{2,1,0:T(8,128)(2,1)} %bitcast.40, bf16[16,16,256]{2,1,0:T(8,128)(2,1)} %param.12), kind=kOutput, calls=%fused_computation.6 | convolution fusion | flops 8404992 | bytes 688128 | tf_op jit(solution)/shard_map/rlq,leq->rle/dot_general | solution.py:57
  1.5 0.0 copy-start.8
  1.5 0.1 reshape.32
  1.6 0.0 copy-start.4
  1.6 1.8 %convolution_convert_fusion.6 = bf16[16,640]{1,0:T(8,128)(2,1)S(1)} fusion(bf16[16,1024]{1,0:T(8,128)(2,1)S(1)} %reshape.32, bf16[640,1024]{1,0:T(8,128)(2,1)} %param.16), kind=kOutput, calls=%fused_computation.10 | convolution fusion | flops 20981760 | bytes 1363968 | tf_op jit(solution)/shard_map/dot_general | solution.py:10
  3.4 0.0 copy-done.3
  3.4 0.0 copy-start.6
  3.4 0.0 slice-start
  3.5 0.2 convolution_convert_fusion.5
  3.6 0.4 copy-done.6
  4.1 0.6 pad_maximum_fusion
  4.7 5.2 %all-to-all-start = ((bf16[4,16,384]{2,1,0:T(8,128)(2,1)}), bf16[4,16,384]{2,1,0:T(8,128)(2,1)S(1)}, u32[]{:S(2)}, u32[]{:S(2)}) async-start(bf16[4,16,384]{2,1,0:T(8,128)(2,1)} %pad_maximum_fusion), calls=%async_computation | async-start | bytes 98304 | tf_op jit(solution)/shard_map/all_to_all | solution.py:21
  9.9 0.0 copy-done.8
  9.9 35.5 %all_gather.6 = bf16[1024,256]{1,0:T(8,128)(2,1)S(1)} all-gather(bf16[64,256]{1,0:T(8,128)(2,1)S(1)} %copy-done.8), channel_id=1, replica_groups={{0,1,2,3,4,5,6,7,8,9,10,11,12,13,14,15},{16,17,18,19,20,21,22,23,24,25,..., dimensions={0}, use_global_device_ids=true | all-gather | bytes 557056 | tf_op jit(solution)/shard_map/all_gather | solution.py:50
  45.5 0.0 copy-done.4
  45.5 0.0 copy-start.5
  45.5 0.2 convolution_convert_fusion.1
  45.7 0.0 all-to-all-done
  45.7 0.0 slice-done
  45.7 0.0 copy-start.7
  45.8 0.1 fusion.2
  45.9 0.5 broadcast.3
  46.4 0.0 slice-start.1
  46.4 0.7 reduce.2
  47.1 0.6 reshape.40
  47.7 0.0 copy-done.7
  47.7 3.5 %all-to-all-start.1 = ((bf16[16,2,384]{2,1,0:T(2,128)(2,1)}), bf16[16,2,384]{2,1,0:T(2,128)(2,1)S(1)}, u32[]{:S(2)}, u32[]{:S(2)}) async-start(bf16[16,2,384]{2,1,0:T(2,128)(2,1)} %reshape.40), calls=%async_computation.1 | async-start | bytes 49152 | tf_op jit(solution)/shard_map/all_to_all | solution.py:21
  51.2 0.0 copy-start.2
  51.3 36.0 %all_gather.7 = bf16[1024,256]{1,0:T(8,128)(2,1)S(1)} all-gather(bf16[64,256]{1,0:T(8,128)(2,1)} %param.23), channel_id=1, replica_groups={{0,1,2,3,4,5,6,7,8,9,10,11,12,13,14,15},{16,17,18,19,20,21,22,23,24,25,..., dimensions={0}, use_global_device_ids=true | all-gather | bytes 557056 | tf_op jit(solution)/shard_map/all_gather | solution.py:53
  87.3 0.0 all-to-all-done.1
  87.3 0.1 convert_reduce_fusion
  87.4 0.7 broadcast_in_dim.10
  88.1 2.6 %all-to-all-start.2 = ((f32[32,1,768]{2,1,0:T(1,128)}), f32[32,1,768]{2,1,0:T(1,128)S(1)}, u32[]{:S(2)}, u32[]{:S(2)}) async-start(f32[32,1,768]{2,1,0:T(1,128)} %broadcast_in_dim.10), calls=%async_computation.2 | async-start | bytes 196608 | tf_op jit(solution)/shard_map/all_to_all | solution.py:88
  90.6 0.0 copy-done.5
  90.7 0.9 convolution_convert_fusion
  91.5 6.7 %all-to-all-done.2 = f32[32,1,768]{2,1,0:T(1,128)S(1)} async-done(((f32[32,1,768]{2,1,0:T(1,128)}), f32[32,1,768]{2,1,0:T(1,128)S(1)}, u32[]{:S(2)}, u32[]{:S(2)}) %all-to-all-start.2) | async-done | bytes 98336 | tf_op jit(solution)/shard_map/all_to_all | solution.py:88
  98.3 0.0 slice-done.1
  98.3 1.0 convolution_convert_fusion.8
  99.2 0.7 broadcast_in_dim.11
  99.9 3.8 %all-to-all-start.3 = ((bf16[4,16,128]{2,1,0:T(8,128)(2,1)}), bf16[4,16,128]{2,1,0:T(8,128)(2,1)}, u32[]{:S(2)}, u32[]{:S(2)}) async-start(bf16[4,16,128]{2,1,0:T(8,128)(2,1)} %broadcast_in_dim.11), calls=%async_computation.3 | async-start | bytes 32768 | tf_op jit(solution)/shard_map/all_to_all | solution.py:21
  103.7 0.0 copy-done
  103.7 0.0 copy-done.2
  103.8 0.0 copy-start.1
  103.8 0.0 slice-start.2
  103.8 1.1 convolution_bitcast_fusion.1
  104.9 0.7 slice.52
  105.6 2.9 %all-to-all-done.3 = bf16[4,16,128]{2,1,0:T(8,128)(2,1)} async-done(((bf16[4,16,128]{2,1,0:T(8,128)(2,1)}), bf16[4,16,128]{2,1,0:T(8,128)(2,1)}, u32[]{:S(2)}, u32[]{:S(2)}) %all-to-all-start.3) | async-done | bytes 16416 | tf_op jit(solution)/shard_map/all_to_all | solution.py:21
  108.5 0.7 copy_bitcast_fusion
  109.2 1.2 %convolution_convert_fusion.7 = bf16[16,256]{1,0:T(8,128)(2,1)S(1)} fusion(bf16[256,768]{1,0:T(8,128)(2,1)} %param.19, bf16[16,512]{1,0:T(8,128)(2,1)S(1)} %copy_bitcast_fusion, bf16[16,256]{1,0:T(8,128)(2,1)S(1)} %slice.52), kind=kOutput, calls=%fused_computation.12 | convolution fusion | flops 6344704 | bytes 425984 | tf_op jit(solution)/shard_map/dot_general | solution.py:10
  110.4 0.0 copy-done.1
  110.4 0.0 slice-done.2
  110.5 0.4 convolution_convert_fusion.3
  110.9 0.1 reshape.37
  111.1 1.3 %fusion = f32[16,16,256]{2,0,1:T(8,128)S(1)} fusion(f32[16,16,256]{2,0,1:T(8,128)} %convolution_bitcast_fusion.1, bf16[16,64,256]{2,1,0:T(8,128)(2,1)} %bitcast.41, bf16[16,16,64]{2,1,0:T(8,128)(2,1)S(1)} %reshape.37), kind=kOutput, calls=%fused_computation.1 | convolution fusion | flops 8454144 | bytes 1081344 | tf_op jit(solution)/shard_map/rle,leq->rlq/dot_general | solution.py:108
  112.4 0.9 copy.47
  (10 shorter events, 0.1 us)
Async XLA Ops:
  0.0 103.7 %copy-start = (bf16[4096,256]{1,0:T(8,128)(2,1)S(1)}, bf16[4096,256]{1,0:T(8,128)(2,1)}, u32[]{:S(2)}) copy-start(bf16[4096,256]{1,0:T(8,128)(2,1)} %param.14) | copy-start | bytes 6291460
  0.0 3.4 %copy-start.3 = (bf16[256,768]{1,0:T(8,128)(2,1)S(1)}, bf16[256,768]{1,0:T(8,128)(2,1)}, u32[]{:S(2)}) copy-start(bf16[256,768]{1,0:T(8,128)(2,1)} %param.18) | copy-start | bytes 1179652
  1.5 8.5 %copy-start.8 = (bf16[64,256]{1,0:T(8,128)(2,1)S(1)}, bf16[64,256]{1,0:T(8,128)(2,1)}, u32[]{:S(2)}) copy-start(bf16[64,256]{1,0:T(8,128)(2,1)} %param.22) | copy-start | bytes 98308
  1.6 43.8 %copy-start.4 = (bf16[128,1536]{1,0:T(8,128)(2,1)S(1)}, bf16[128,1536]{1,0:T(8,128)(2,1)}, u32[]{:S(2)}) copy-start(bf16[128,1536]{1,0:T(8,128)(2,1)} %param.20) | copy-start | bytes 1179652
  3.4 0.6 copy-start.6
  3.4 42.3 %slice-start = ((bf16[128,1536]{1,0:T(8,128)(2,1)}), bf16[128,512]{1,0:T(8,128)(2,1)S(1)}, s32[]{:S(2)}) async-start(bf16[128,1536]{1,0:T(8,128)(2,1)} %param.20), calls=%async_computation.4 | async-start | bytes 262144 | tf_op jit(solution)/shard_map/slice | solution.py:82
  4.7 41.0 %all-to-all-start = ((bf16[4,16,384]{2,1,0:T(8,128)(2,1)}), bf16[4,16,384]{2,1,0:T(8,128)(2,1)S(1)}, u32[]{:S(2)}, u32[]{:S(2)}) async-start(bf16[4,16,384]{2,1,0:T(8,128)(2,1)} %pad_maximum_fusion), calls=%async_computation | async-start | bytes 98304 | tf_op jit(solution)/shard_map/all_to_all | solution.py:21
  45.5 45.2 %copy-start.5 = (bf16[128,1536]{1,0:T(8,128)(2,1)S(1)}, bf16[128,1536]{1,0:T(8,128)(2,1)}, u32[]{:S(2)}) copy-start(bf16[128,1536]{1,0:T(8,128)(2,1)} %param.21) | copy-start | bytes 1179652
  45.7 2.0 %copy-start.7 = (bf16[16,384]{1,0:T(8,128)(2,1)}, bf16[16,384]{1,0:T(8,128)(2,1)S(1)}, u32[]{:S(2)}) copy-start(bf16[16,384]{1,0:T(8,128)(2,1)S(1)} %reduce_sum.30) | copy-start | bytes 36868
  46.4 51.8 %slice-start.1 = ((bf16[128,1536]{1,0:T(8,128)(2,1)}), bf16[128,512]{1,0:T(8,128)(2,1)S(1)}, s32[]{:S(2)}) async-start(bf16[128,1536]{1,0:T(8,128)(2,1)} %param.21), calls=%async_computation.5 | async-start | bytes 262144 | tf_op jit(solution)/shard_map/slice | solution.py:98
  47.7 39.5 %all-to-all-start.1 = ((bf16[16,2,384]{2,1,0:T(2,128)(2,1)}), bf16[16,2,384]{2,1,0:T(2,128)(2,1)S(1)}, u32[]{:S(2)}, u32[]{:S(2)}) async-start(bf16[16,2,384]{2,1,0:T(2,128)(2,1)} %reshape.40), calls=%async_computation.1 | async-start | bytes 49152 | tf_op jit(solution)/shard_map/all_to_all | solution.py:21
  51.2 52.5 %copy-start.2 = (bf16[16,16,256]{2,1,0:T(8,128)(2,1)S(1)}, bf16[16,16,256]{2,1,0:T(8,128)(2,1)}, u32[]{:S(2)}) copy-start(bf16[16,16,256]{2,1,0:T(8,128)(2,1)} %param.12) | copy-start | bytes 393220
  88.1 10.1 %all-to-all-start.2 = ((f32[32,1,768]{2,1,0:T(1,128)}), f32[32,1,768]{2,1,0:T(1,128)S(1)}, u32[]{:S(2)}, u32[]{:S(2)}) async-start(f32[32,1,768]{2,1,0:T(1,128)} %broadcast_in_dim.10), calls=%async_computation.2 | async-start | bytes 196608 | tf_op jit(solution)/shard_map/all_to_all | solution.py:88
  99.9 8.6 %all-to-all-start.3 = ((bf16[4,16,128]{2,1,0:T(8,128)(2,1)}), bf16[4,16,128]{2,1,0:T(8,128)(2,1)}, u32[]{:S(2)}, u32[]{:S(2)}) async-start(bf16[4,16,128]{2,1,0:T(8,128)(2,1)} %broadcast_in_dim.11), calls=%async_computation.3 | async-start | bytes 32768 | tf_op jit(solution)/shard_map/all_to_all | solution.py:21
  103.8 6.6 %copy-start.1 = (bf16[1024,640]{1,0:T(8,128)(2,1)S(1)}, bf16[1024,640]{1,0:T(8,128)(2,1)}, u32[]{:S(2)}) copy-start(bf16[1024,640]{1,0:T(8,128)(2,1)} %param.17) | copy-start | bytes 3932164
  103.8 6.6 %slice-start.2 = ((bf16[16,640]{1,0:T(8,128)(2,1)}), bf16[16,384]{1,0:T(8,128)(2,1)S(1)}, s32[]{:S(2)}) async-start(bf16[16,640]{1,0:T(8,128)(2,1)} %copy-done.6), calls=%async_computation.6 | async-start | bytes 24576 | tf_op jit(solution)/shard_map/slice | solution.py:104

commit v2 on v1

v2 whole, which is shorter than its diff:
```python
import jax
import jax.numpy as jnp
from jax import lax
from jax.sharding import PartitionSpec as P

AXES = ("gx", "gy")


def contract(left, right):
    return lax.dot_general(
        left, right, (((1,), (1,)), ((), ())), preferred_element_type=jnp.float32
    )


def product(left, right):
    return jnp.dot(left, right, preferred_element_type=jnp.float32)


def partner_sum(term, bit):
    count = lax.axis_size(AXES)
    other = lax.ppermute(term.astype(jnp.bfloat16), AXES, [(i, i ^ bit) for i in range(count)])
    return term + other.astype(jnp.float32)


def gathered(block, size):
    count = lax.axis_size(AXES)
    groups = [list(range(start, start + size)) for start in range(0, count, size)]
    return lax.all_gather(block, AXES, axis_index_groups=groups, tiled=True)


def per_device(
    source,
    leaf_flux,
    leaf_particular,
    leaf_lift,
    box_up,
    box_down,
    up_one,
    down_one,
    up_two,
    down_two,
    up_root,
    down_root,
):
    rhs_count, leaves, points = source.shape
    edge_count = leaf_flux.shape[0] // leaves
    count = lax.axis_size(AXES)
    k_zero = up_one.shape[0]
    inner_dev = box_up.shape[0] - k_zero
    k_one = up_one.shape[1] - k_zero
    quad = k_one // up_two.shape[0]
    family = (up_two.shape[1] - k_one) // up_root.shape[0]
    root_points = up_root.shape[1]

    up_two_box = gathered(up_two, quad)
    roots = gathered(jnp.concatenate([up_root, down_root], axis=1), family)
    down_two_box = gathered(down_two, quad)

    flux = jnp.einsum(
        "rlq,leq->rle",
        source,
        leaf_flux.reshape(leaves, edge_count, points),
        preferred_element_type=jnp.float32,
    )
    flux = flux.astype(jnp.bfloat16).reshape(rhs_count, leaves * edge_count)
    box_state = contract(flux, box_up).astype(jnp.bfloat16)
    first_sum = product(box_state[:, inner_dev:], up_one)
    bit = 1
    while bit < quad:
        first_sum = partner_sum(first_sum, bit)
        bit *= 2
    first_state = first_sum.astype(jnp.bfloat16)

    second_term = product(first_state[:, k_zero:], up_two_box)
    root_term = product(second_term[:, k_one:].astype(jnp.bfloat16), roots[:, :root_points])
    total = jnp.concatenate([second_term[:, :k_one], root_term], axis=1)
    while bit < family:
        total = partner_sum(total, bit)
        bit *= 2
    second_inner = total[:, :k_one].astype(jnp.bfloat16)
    root_sum = total[:, k_one:]
    while bit < count:
        root_sum = partner_sum(root_sum, bit)
        bit *= 2
    root_state = root_sum.astype(jnp.bfloat16)

    top_bound = contract(root_state, roots[:, root_points:]).astype(jnp.bfloat16)
    second_input = jnp.concatenate([second_inner, top_bound], axis=1)
    mid_bound = contract(second_input, down_two_box).astype(jnp.bfloat16)
    first_input = jnp.concatenate([first_state[:, :k_zero], mid_bound], axis=1)
    box_bound = contract(first_input, down_one).astype(jnp.bfloat16)
    box_input = jnp.concatenate([box_state[:, :inner_dev], box_bound], axis=1)
    leaf_bound = (
        contract(box_input, box_down).astype(jnp.bfloat16).reshape(rhs_count, leaves, edge_count)
    )
    lifted = jnp.einsum(
        "rle,leq->rlq",
        leaf_bound,
        leaf_lift.reshape(leaves, edge_count, points),
        preferred_element_type=jnp.float32,
    )
    particular = jnp.einsum(
        "rlq,lqp->rlp",
        source,
        leaf_particular.reshape(leaves, points, points),
        preferred_element_type=jnp.float32,
    )
    return lifted + particular


def solution(mesh):
    return jax.shard_map(
        per_device,
        mesh=mesh,
        in_specs=(P(None, AXES, None),) + (P(AXES, None),) * 11,
        out_specs=P(None, AXES, None),
        check_vma=False,
    )
```

time: 114 us -> 135 us (1.18)
  waiting for transfers between devices: 9.64 us -> 100 us
  blocking collectives: 71.5 us -> 0 us
  between operations: 0.3 us -> 13.2 us
  starting transfers between devices: 15.1 us -> 7.69 us
  local copies, waits for them, and re-layouts: 5.6 us -> 1.22 us
  matrix products: 9.61 us -> 11.1 us
    all_gather x0 -> x3, waiting for transfers between devices: none -> 88.9 us  [gathered(): return lax.all_gather(block, AXES, axis_index_groups=groups, tiled=True)]
    all_gather x2 -> x0, blocking collectives: 71.5 us -> none  [the longest x1 36 us: per_device(): lax.all_gather(down_root, AXES, axis_index_groups=groups_of(family), tile...]
    all_to_all x4 -> x0, starting transfers between devices: 15.1 us -> none  [the longest x3 12.6 us: swap(): return lax.all_to_all(pieces, AXES, 0, 0, axis_index_groups=groups_of(size))]
    ppermute x0 -> x5, waiting for transfers between devices: none -> 10 us  [partner_sum(): lax.ppermute(term.astype(jnp.bfloat16), AXES, [(i, i ^ bit) for i in rang...]
    all_to_all x4 -> x0, waiting for transfers between devices: 9.64 us -> none  [the longest x1 6.69 us: per_device(): lax.all_to_all(jnp.broadcast_to(second_rows, (count,) + second_rows.shape...]
    ppermute x0 -> x5, starting transfers between devices: none -> 7.61 us  [partner_sum(): lax.ppermute(term.astype(jnp.bfloat16), AXES, [(i, i ^ bit) for i in rang...]
    dot_general x4 -> x3, matrix products: 1.39 us -> 4.13 us  [product(): return jnp.dot(left, right, preferred_element_type=jnp.float32)]
    unnamed x0 -> x3, waiting for transfers between devices: none -> 1.41 us
  transfers between devices with their start and end apart: 4 -> 8, of which waited for: 2 -> 8; matrix products, arithmetic and copies ran while one was open for 3% -> 7% of each run, Pallas kernels for 0% -> 0%
where the time goes in v2:
time: 135 us
  waiting for transfers between devices  100 us (74%)
  between operations  13.2 us (10%)
  matrix products  11.1 us (8%)
  starting transfers between devices  7.69 us (6%)
  other arithmetic  1.46 us (1%)
    all_gather x3, waiting for transfers between devices, gathered(): return lax.all_gather(block, AXES, axis_index_groups=groups, tiled=True)  88.9 us
    ppermute x5, waiting for transfers between devices, partner_sum(): lax.ppermute(term.astype(jnp.bfloat16), AXES, [(i, i ^ bit) for i in rang...  10 us
    ppermute x5, starting transfers between devices, partner_sum(): lax.ppermute(term.astype(jnp.bfloat16), AXES, [(i, i ^ bit) for i in rang...  7.61 us
    dot_general x3, matrix products, product(): return jnp.dot(left, right, preferred_element_type=jnp.float32)  4.13 us
    dot_general x5, matrix products, contract(): lax.dot_general(left, right, (((1,), (1,)), ((), ())), preferred_element_...  3.31 us
  transfers between devices with their start and end apart: 8, of which 8 were waited for; matrix products, arithmetic and copies ran while one was open for 7% of the time, Pallas kernels for 0%

profile of v2, /device:TPU:0, one launch (start us, length us, event | category | flops | bytes accessed | tf_op | source)
XLA Modules:
  0.0 135.0 jit_solution(17889200251365300451)
XLA Ops:
  6.5 0.0 copy-start
  6.5 0.0 copy-start.1
  6.5 0.0 all-gather.4.cloned.1.call-start
  6.5 0.7 all-gather.4.cloned.1.call-update
  7.3 0.0 all-gather.6.cloned.1.call-start
  7.3 1.4 %pad_maximum_fusion = bf16[64,512]{1,0:T(8,128)(2,1)} fusion(bf16[64,256]{1,0:T(8,128)(2,1)} %param.23, bf16[64,256]{1,0:T(8,128)(2,1)} %param.22), kind=kLoop, calls=%fused_computation.16 | loop fusion | flops 131072 | bytes 131072 | tf_op jit(solution)/shard_map/concatenate | solution.py:56
  8.7 0.0 all-gather.6.cloned.1.call-update
  8.7 0.0 all-gather.8.cloned.1.call-start
  8.8 0.7 all-gather.8.cloned.1.call-update
  9.5 1.3 fusion.1
  10.8 0.1 reshape.16
  10.9 0.0 copy-done.1
  10.9 0.4 convolution_convert_fusion.3
  11.4 0.0 copy-start.7
  11.4 1.2 fusion.27
  12.6 0.0 copy-start.4
  12.6 3.0 %collective-permute-start = (bf16[16,768]{1,0:T(8,128)(2,1)S(1)}, bf16[16,768]{1,0:T(8,128)(2,1)S(1)}, u32[]{:S(2)}, u32[]{:S(2)}) collective-permute-start(bf16[16,768]{1,0:T(8,128)(2,1)S(1)} %get-tuple-element.5), channel_id=1, source_target_pairs={{0,1},{1,0},{2,3},{3,2},{4,5},{5,4},{6,7},{7,6},{8,9},{9,8},{10,11... | collective-permute-start | bytes 73736 | tf_op jit(solution)/shard_map/ppermute | solution.py:21
  15.6 1.8 %collective-permute-done = bf16[16,768]{1,0:T(8,128)(2,1)S(1)} collective-permute-done((bf16[16,768]{1,0:T(8,128)(2,1)S(1)}, bf16[16,768]{1,0:T(8,128)(2,1)S(1)}, u32[]{:S(2)}, u32[]{:S(2)}) %collective-permute-start) | collective-permute-done | bytes 24608 | tf_op jit(solution)/shard_map/ppermute | solution.py:21
  17.4 2.1 %collective-permute-start.1 = (bf16[16,768]{1,0:T(8,128)(2,1)S(1)}, bf16[16,768]{1,0:T(8,128)(2,1)S(1)}, u32[]{:S(2)}, u32[]{:S(2)}) collective-permute-start(bf16[16,768]{1,0:T(8,128)(2,1)S(1)} %fusion.12), channel_id=1, source_target_pairs={{0,2},{1,3},{2,0},{3,1},{4,6},{5,7},{6,4},{7,5},{8,10},{9,11},{10,... | collective-permute-start | bytes 73736 | tf_op jit(solution)/shard_map/ppermute | solution.py:21
  19.6 1.8 %collective-permute-done.1 = bf16[16,768]{1,0:T(8,128)(2,1)S(1)} collective-permute-done((bf16[16,768]{1,0:T(8,128)(2,1)S(1)}, bf16[16,768]{1,0:T(8,128)(2,1)S(1)}, u32[]{:S(2)}, u32[]{:S(2)}) %collective-permute-start.1) | collective-permute-done | bytes 24608 | tf_op jit(solution)/shard_map/ppermute | solution.py:21
  21.4 0.0 copy-start.6
  21.4 25.8 %all-gather.4.cloned.1.call-done = bf16[512,1536]{1,0:T(8,128)(2,1)} async-done(((bf16[128,1536]{1,0:T(8,128)(2,1)}), bf16[512,1536]{1,0:T(8,128)(2,1)}) %all-gather.4.cloned.1.call-update) | async-done | bytes 1572880 | tf_op jit(solution)/shard_map/all_gather | solution.py:28
  47.2 1.7 %fusion.20 = f32[16,1536]{1,0:T(8,128)S(1)} fusion(bf16[512,1536]{1,0:T(8,128)(2,1)} %all-gather.4.cloned.1.call-done, bf16[16,768]{1,0:T(8,128)(2,1)S(1)} %add_convert_fusion), kind=kOutput, calls=%fused_computation.36 | convolution fusion | flops 25165824 | bytes 1687552 | tf_op jit(solution)/shard_map/dot_general | solution.py:16
  49.0 38.5 %all-gather.6.cloned.1.call-done = bf16[1024,512]{1,0:T(8,128)(2,1)} async-done(((bf16[64,512]{1,0:T(8,128)(2,1)}), bf16[1024,512]{1,0:T(8,128)(2,1)}) %all-gather.6.cloned.1.call-update) | async-done | bytes 1048592 | tf_op jit(solution)/shard_map/all_gather | solution.py:28
  87.4 1.2 fusion.3
  88.6 0.0 copy-start.3
  88.7 0.8 collective-permute-start.2
  89.5 4.2 %collective-permute-done.2 = bf16[16,768]{1,0:T(8,128)(2,1)S(1)} collective-permute-done((bf16[16,768]{1,0:T(8,128)(2,1)S(1)}, bf16[16,768]{1,0:T(8,128)(2,1)S(1)}, u32[]{:S(2)}, u32[]{:S(2)}) %collective-permute-start.2) | collective-permute-done | bytes 24608 | tf_op jit(solution)/shard_map/ppermute | solution.py:21
  93.7 0.1 collective-permute-start.3
  93.7 1.2 collective-permute-done.3
  95.0 1.5 %collective-permute-start.4 = (bf16[16,256]{1,0:T(8,128)(2,1)S(1)}, bf16[16,256]{1,0:T(8,128)(2,1)S(1)}, u32[]{:S(2)}, u32[]{:S(2)}) collective-permute-start(bf16[16,256]{1,0:T(8,128)(2,1)S(1)} %slice.67), channel_id=1, source_target_pairs={{0,16},{1,17},{2,18},{3,19},{4,20},{5,21},{6,22},{7,23},{8,24},{9,... | collective-permute-start | bytes 24584 | tf_op jit(solution)/shard_map/ppermute | solution.py:21
  96.5 0.0 copy-done
  96.5 0.0 copy-done.4
  96.5 1.1 convolution_bitcast_fusion.1
  97.6 0.0 copy-done.7
  97.6 0.0 copy-start.2
  97.6 0.0 copy-done.6
  97.6 0.0 slice-start.1
  97.6 0.0 slice-start
  97.6 1.0 collective-permute-done.4
  98.7 0.0 copy-done.3
  98.7 0.2 convolution_convert_fusion.2
  98.9 24.6 %all-gather.8.cloned.1.call-done = bf16[512,1536]{1,0:T(8,128)(2,1)} async-done(((bf16[128,1536]{1,0:T(8,128)(2,1)}), bf16[512,1536]{1,0:T(8,128)(2,1)}) %all-gather.8.cloned.1.call-update) | async-done | bytes 1572880 | tf_op jit(solution)/shard_map/all_gather | solution.py:28
  123.5 0.0 copy-start.5
  123.5 2.0 %convolution_convert_fusion.4 = bf16[16,512]{1,0:T(8,128)(2,1)S(1)} fusion(bf16[512,1536]{1,0:T(8,128)(2,1)} %all-gather.8.cloned.1.call-done, bf16[16,1024]{1,0:T(8,128)(2,1)S(1)} %convolution_convert_fusion.2, bf16[16,512]{1,0:T(8,128)(2,1)S(1)} %slice.66), kind=kOutput, calls=%fused_computation.8 | convolution fusion | flops 25272320 | bytes 1638400 | tf_op jit(solution)/shard_map/dot_general | solution.py:10
  125.5 0.0 slice-done
  125.5 0.0 copy-done.5
  125.5 0.2 convolution_convert_fusion.5
  125.7 0.0 copy-done.2
  125.7 0.0 slice-done.1
  125.7 0.5 convolution_convert_fusion.1
  126.2 0.1 reshape.17
  126.3 1.3 fusion
  127.6 0.9 copy.21
  (9 shorter events, 0.1 us)
Async XLA Ops:
  6.5 90.0 %copy-start = (bf16[4096,256]{1,0:T(8,128)(2,1)S(1)}, bf16[4096,256]{1,0:T(8,128)(2,1)}, u32[]{:S(2)}) copy-start(bf16[4096,256]{1,0:T(8,128)(2,1)} %param.14) | copy-start | bytes 6291460
  6.5 4.4 %copy-start.1 = (bf16[640,1024]{1,0:T(8,128)(2,1)S(1)}, bf16[640,1024]{1,0:T(8,128)(2,1)}, u32[]{:S(2)}) copy-start(bf16[640,1024]{1,0:T(8,128)(2,1)} %param.16) | copy-start | bytes 3932164
  6.5 40.7 %all-gather.4.cloned.1.call-start = ((), (), s32[]{:S(2)}) async-start(), calls=%async_computation | async-start | bytes 1966080 | tf_op jit(solution)/shard_map/all_gather | solution.py:28
  7.3 80.2 %all-gather.6.cloned.1.call-start = ((), (), s32[]{:S(2)}) async-start(), calls=%async_computation.1 | async-start | bytes 1114112 | tf_op jit(solution)/shard_map/all_gather | solution.py:28
  8.7 114.8 %all-gather.8.cloned.1.call-start = ((), (), s32[]{:S(2)}) async-start(), calls=%async_computation.2 | async-start | bytes 1966080 | tf_op jit(solution)/shard_map/all_gather | solution.py:28
  11.4 86.2 %copy-start.7 = (bf16[16,640]{1,0:T(8,128)(2,1)}, bf16[16,640]{1,0:T(8,128)(2,1)S(1)}, u32[]{:S(2)}) copy-start(bf16[16,640]{1,0:T(8,128)(2,1)S(1)} %convolution_convert_fusion.3) | copy-start | bytes 61444
  12.6 83.9 %copy-start.4 = (bf16[16,16,256]{2,1,0:T(8,128)(2,1)S(1)}, bf16[16,16,256]{2,1,0:T(8,128)(2,1)}, u32[]{:S(2)}) copy-start(bf16[16,16,256]{2,1,0:T(8,128)(2,1)} %param.12) | copy-start | bytes 393220
  12.6 4.8 %collective-permute-start = (bf16[16,768]{1,0:T(8,128)(2,1)S(1)}, bf16[16,768]{1,0:T(8,128)(2,1)S(1)}, u32[]{:S(2)}, u32[]{:S(2)}) collective-permute-start(bf16[16,768]{1,0:T(8,128)(2,1)S(1)} %get-tuple-element.5), channel_id=1, source_target_pairs={{0,1},{1,0},{2,3},{3,2},{4,5},{5,4},{6,7},{7,6},{8,9},{9,8},{10,11... | collective-permute-start | bytes 73736 | tf_op jit(solution)/shard_map/ppermute | solution.py:21
  17.4 3.9 %collective-permute-start.1 = (bf16[16,768]{1,0:T(8,128)(2,1)S(1)}, bf16[16,768]{1,0:T(8,128)(2,1)S(1)}, u32[]{:S(2)}, u32[]{:S(2)}) collective-permute-start(bf16[16,768]{1,0:T(8,128)(2,1)S(1)} %fusion.12), channel_id=1, source_target_pairs={{0,2},{1,3},{2,0},{3,1},{4,6},{5,7},{6,4},{7,5},{8,10},{9,11},{10,... | collective-permute-start | bytes 73736 | tf_op jit(solution)/shard_map/ppermute | solution.py:21
  21.4 76.2 %copy-start.6 = (bf16[16,768]{1,0:T(8,128)(2,1)}, bf16[16,768]{1,0:T(8,128)(2,1)S(1)}, u32[]{:S(2)}) copy-start(bf16[16,768]{1,0:T(8,128)(2,1)S(1)} %add_convert_fusion) | copy-start | bytes 73732
  88.6 10.0 %copy-start.3 = (bf16[1024,512]{1,0:T(8,128)(2,1)S(1)}, bf16[1024,512]{1,0:T(8,128)(2,1)}, u32[]{:S(2)}) copy-start(bf16[1024,512]{1,0:T(8,128)(2,1)} %all-gather.6.cloned.1.call-done) | copy-start | bytes 3145732
  88.7 5.0 %collective-permute-start.2 = (bf16[16,768]{1,0:T(8,128)(2,1)S(1)}, bf16[16,768]{1,0:T(8,128)(2,1)S(1)}, u32[]{:S(2)}, u32[]{:S(2)}) collective-permute-start(bf16[16,768]{1,0:T(8,128)(2,1)S(1)} %fusion.11), channel_id=1, source_target_pairs={{0,4},{1,5},{2,6},{3,7},{4,0},{5,1},{6,2},{7,3},{8,12},{9,13},{10,... | collective-permute-start | bytes 73736 | tf_op jit(solution)/shard_map/ppermute | solution.py:21
  93.7 1.3 collective-permute-start.3
  95.0 3.7 %collective-permute-start.4 = (bf16[16,256]{1,0:T(8,128)(2,1)S(1)}, bf16[16,256]{1,0:T(8,128)(2,1)S(1)}, u32[]{:S(2)}, u32[]{:S(2)}) collective-permute-start(bf16[16,256]{1,0:T(8,128)(2,1)S(1)} %slice.67), channel_id=1, source_target_pairs={{0,16},{1,17},{2,18},{3,19},{4,20},{5,21},{6,22},{7,23},{8,24},{9,... | collective-permute-start | bytes 24584 | tf_op jit(solution)/shard_map/ppermute | solution.py:21
  97.6 28.1 %copy-start.2 = (bf16[1024,640]{1,0:T(8,128)(2,1)S(1)}, bf16[1024,640]{1,0:T(8,128)(2,1)}, u32[]{:S(2)}) copy-start(bf16[1024,640]{1,0:T(8,128)(2,1)} %param.17) | copy-start | bytes 3932164
  97.6 28.1 %slice-start.1 = ((bf16[16,640]{1,0:T(8,128)(2,1)}), bf16[16,384]{1,0:T(8,128)(2,1)S(1)}, s32[]{:S(2)}) async-start(bf16[16,640]{1,0:T(8,128)(2,1)} %copy-done.7), calls=%async_computation.4 | async-start | bytes 24576 | tf_op jit(solution)/shard_map/slice | solution.py:92
  97.6 27.9 %slice-start = ((bf16[16,768]{1,0:T(8,128)(2,1)}), bf16[16,256]{1,0:T(8,128)(2,1)S(1)}, s32[]{:S(2)}) async-start(bf16[16,768]{1,0:T(8,128)(2,1)} %copy-done.6), calls=%async_computation.3 | async-start | bytes 16384 | tf_op jit(solution)/shard_map/slice | solution.py:90
  123.5 2.0 %copy-start.5 = (bf16[256,768]{1,0:T(8,128)(2,1)S(1)}, bf16[256,768]{1,0:T(8,128)(2,1)}, u32[]{:S(2)}) copy-start(bf16[256,768]{1,0:T(8,128)(2,1)} %param.19) | copy-start | bytes 1179652
Sparse Core Ops, SparseCore 0:
  8.9 38.2 all-gather.3
  49.4 37.9 all-gather.5
  89.0 34.4 all-gather.7
